TPU v7x, 32 devices: a whole 2x2x4 slice. The times are simulated.
32 devices in a mesh: occ: 4 (over x, core), vir: 8 (over z, y).
Axes of the slice: x: 2, y: 2, z: 4, core: 2. Of those that a mesh axis runs over, the one named last changes fastest.
Arguments:
- amplitudes: bfloat16 [4, 2, 4096, 4096], P('occ', None, None, 'vir'), may hold values from -6 to 6
- coulomb: bfloat16 [4, 2, 4096, 4096], P('occ', None, None, 'vir'), may hold values from -6 to 6
- ladder_tiles: bfloat16 [256, 128, 128], P('vir'), may hold values from -0.1875 to 0.1875
- cycle_tiles: bfloat16 [256, 128, 128], P('vir'), may hold values from -0.25 to 0.25
- ladder_screen: int32 [32, 8], replicated, may hold values from 0 to 31, as said below
- tile_slot: int32 [256], replicated, may hold values from 0 to 255, each once
- cycle_screen: int32 [64, 4], replicated, may hold values from 0 to 63, as said below
- cycle_rows: int32 [32, 48], replicated, may hold values from 0 to 63, as said below
- cycle_count: int32 [32], replicated, may hold values from 1 to 48, 1024 in all
- slab_occ: int32 [4], replicated, may hold values from 0 to 399
- window_occ: int32 [2], replicated, may hold values from 0 to 399
- occ_energy: float32 [400], replicated, may hold values from -3 to -0.5
- vir_energy: float32 [4096], replicated, may hold values from 0.4 to 4
Outputs:
- updated: bfloat16 [4, 2, 4096, 4096], P('occ', None, None, 'vir')
Inputs may be any that keep to these rules, and one draw needn't show every extreme that they name: `ladder_screen`: each row names 8 different tiles. `cycle_screen`: each row names 4 different row tiles. `cycle_rows`: each row names 48 different block columns; the first cycle_count of them are used. `cycle_count`: the counts sum to exactly 1024, and the largest is exactly 48.
All inputs are finite; a program needn't handle non-finite values.
Results may differ from a plain program's by a relative error of at most 0.003.
Values may be sent and summed in bfloat16 or wider, within the bound.
A program may use at most 192 MiB of HBM per device.

v0:
```python
import math

import jax
import jax.numpy as jnp
from jax import lax
from jax.sharding import PartitionSpec as P


def body(
    amplitudes,
    coulomb,
    ladder_tiles,
    cycle_tiles,
    ladder_screen,
    tile_slot,
    cycle_screen,
    cycle_rows,
    cycle_count,
    slab_occ,
    window_occ,
    occ_energy,
    vir_energy,
):
    occ_count = lax.axis_size("occ")
    vir_count = lax.axis_size("vir")
    dev_count = occ_count * vir_count
    slab_rows, window, width_all, block_cols = amplitudes.shape
    tile_side = ladder_tiles.shape[1]
    tile_count = width_all // tile_side
    ladder_keep = ladder_screen.shape[1]
    cycle_keep = cycle_screen.shape[1]
    column_tiles = cycle_screen.shape[0]
    rows_here = width_all // dev_count
    slab_all = slab_rows * occ_count
    all_ladder, all_cycle = (
        lax.all_gather(ladder_tiles, "vir", axis=0, tiled=True),
        lax.all_gather(cycle_tiles, "vir", axis=0, tiled=True),
    )
    front, inner = (1, rows_here)
    split = amplitudes.reshape(slab_rows, window, front, occ_count, vir_count, inner, block_cols)
    flat = split.reshape(1, slab_rows, window, front, dev_count, inner, block_cols)
    moved = lax.all_to_all(flat, ("occ", "vir"), split_axis=4, concat_axis=0, tiled=True)
    moved = moved.reshape(occ_count, vir_count, slab_rows, window, front, inner, block_cols)
    moved = moved.transpose(0, 2, 3, 4, 5, 1, 6)
    cycle_amp = moved.reshape(slab_all, window, front * inner, width_all)
    extent = slab_rows * window * block_cols
    arranged = amplitudes.transpose(2, 0, 1, 3).reshape(tile_count, tile_side, extent)
    slots = tile_slot.reshape(tile_count, ladder_keep)
    group = math.gcd(tile_count, 8)

    def ladder_block(start):
        screen_part = lax.dynamic_slice_in_dim(ladder_screen, start, group, 0)
        slot_part = lax.dynamic_slice_in_dim(slots, start, group, 0)
        picked_rows = arranged[screen_part]
        weights = all_ladder[slot_part]
        return jnp.einsum(
            "akrc,akce->are", weights, picked_rows, preferred_element_type=jnp.float32
        )

    starts = jnp.arange(0, tile_count, group, dtype=jnp.int32)
    total = lax.map(ladder_block, starts)
    ladder = total.reshape(width_all, slab_rows, window, block_cols).transpose(1, 2, 0, 3)
    source = cycle_amp.reshape(slab_all, window, front, inner, tile_count, tile_side)
    source = source.transpose(1, 4, 2, 0, 3, 5).reshape(
        window * tile_count, front, slab_all * inner, tile_side
    )
    cycle_sel = all_cycle.reshape(column_tiles, cycle_keep, tile_side, tile_side)
    device = lax.axis_index("occ") * vir_count + lax.axis_index("vir")
    my_tile = device * rows_here // tile_side
    columns = lax.dynamic_index_in_dim(cycle_rows, my_tile, 0, keepdims=False)
    used = lax.dynamic_index_in_dim(cycle_count, my_tile, 0, keepdims=False)
    valid = jnp.arange(columns.shape[0], dtype=jnp.int32) < used
    picked = source[cycle_screen[columns], 0]
    part = jnp.einsum(
        "emrc,emcb->erb", picked, cycle_sel[columns], preferred_element_type=jnp.float32
    )
    part = jnp.where(valid[:, None, None], part, 0.0)
    placed = (
        jnp.zeros((column_tiles, slab_all * inner, tile_side), jnp.float32).at[columns].add(part)
    )
    cycle_cols = placed.reshape(column_tiles, front, slab_all * inner, tile_side)
    cycle_cols = cycle_cols.astype(jnp.bfloat16).reshape(
        window, tile_count, front, slab_all, inner, tile_side
    )
    cycle_view = cycle_cols.transpose(3, 0, 2, 4, 1, 5).reshape(
        slab_all, window, front * inner, width_all
    )
    shaped = cycle_view.reshape(occ_count, slab_rows, window, front, inner, vir_count, block_cols)
    shaped = shaped.transpose(0, 5, 1, 2, 3, 4, 6).reshape(
        dev_count, slab_rows, window, front, 1, inner, block_cols
    )
    back = lax.all_to_all(shaped, ("occ", "vir"), split_axis=0, concat_axis=4, tiled=True)
    cycle = back.reshape(slab_rows, window, width_all, block_cols)
    occ_total = occ_energy.shape[0]
    orbital_ids = jnp.arange(occ_total, dtype=jnp.int32)
    my_slab = lax.dynamic_slice_in_dim(slab_occ, lax.axis_index("occ") * slab_rows, slab_rows)
    energy_i = jnp.sum(
        jnp.where(my_slab[:, None] == orbital_ids[None, :], occ_energy[None, :], 0.0), axis=1
    )
    energy_j = jnp.sum(
        jnp.where(window_occ[:, None] == orbital_ids[None, :], occ_energy[None, :], 0.0), axis=1
    )
    energy_b = lax.dynamic_slice_in_dim(vir_energy, lax.axis_index("vir") * block_cols, block_cols)
    denominator = (
        vir_energy[None, None, :, None]
        + energy_b[None, None, None, :]
        - energy_i[:, None, None, None]
        - energy_j[None, :, None, None]
    )
    value = coulomb.astype(jnp.float32) + ladder + cycle.astype(jnp.float32)
    return (value / denominator).astype(jnp.bfloat16)


def solution(mesh):
    return jax.shard_map(
        body,
        mesh=mesh,
        in_specs=(
            P("occ", None, None, "vir"),
            P("occ", None, None, "vir"),
            P("vir", None, None),
            P("vir", None, None),
            P(),
            P(),
            P(),
            P(),
            P(),
            P(),
            P(),
            P(),
            P(),
        ),
        out_specs=P("occ", None, None, "vir"),
        check_vma=False,
    )
```

profile of v0, /device:TPU:14, one launch (start us, length us, event | category | flops | bytes accessed | tf_op | source)
XLA Modules:
  0.0 742.6 jit_solution(7589579825542692193)
XLA Ops:
  6.5 0.7 all-gather.5.cloned.1.call-update
  7.3 7.8 %copy.64 = bf16[1,1,2,1,32,128,512]{6,5,2,3,1,0,4:T(8,128)(2,1)} copy(bf16[1,1,2,1,32,128,512]{6,5,4,2,3,1,0:T(8,128)(2,1)} %bitcast.85) | data formatting | bytes 16777216 | tf_op jit(solution)/shard_map/reshape;reshape | solution.py:41
  15.0 6.0 all-to-all-start
  21.1 0.7 all-gather.3.cloned.1.call-update
  21.8 0.1 copy.67
  21.9 0.6 dynamic_slice.25
  22.6 0.7 fusion.6
  23.3 0.6 gather_fusion.2
  23.9 0.1 reshape.181
  24.0 0.6 iota_compare_fusion.1
  24.6 249.7 %all-gather.5.cloned.1.call-done = bf16[256,128,128]{2,1,0:T(8,128)(2,1)} async-done(((bf16[32,128,128]{2,1,0:T(8,128)(2,1)}), bf16[256,128,128]{2,1,0:T(8,128)(2,1)}) %all-gather.5.cloned.1.call-update) | async-done | bytes 8388624 | tf_op jit(solution)/shard_map/all_gather | solution.py:37
  274.4 8.3 %gather_fusion.4 = bf16[48,4,128,128]{3,2,1,0:T(8,128)(2,1)} fusion(bf16[64,4,128,128]{3,2,1,0:T(8,128)(2,1)} %bitcast.91, s32[1024]{0:T(1024)S(1)} %pad_clamp_fusion.2), kind=kCustom, calls=%fused_computation.4 | custom fusion | bytes 12583104 | tf_op jit(solution)/shard_map/gather | solution.py:75
  282.6 33.9 %all-to-all-done = bf16[1,1,2,1,32,128,512]{6,5,2,3,1,0,4:T(8,128)(2,1)} async-done(((bf16[1,1,2,1,32,128,512]{6,5,2,3,1,0,4:T(8,128)(2,1)}), bf16[1,1,2,1,32,128,512]{6,5,2,3,1,0,4:T(8,128)(2,1)}, u32[]{:S(2)}, u32[]{:S(2)}) %all-to-all-start) | async-done | bytes 8388640 | tf_op jit(solution)/shard_map/all_to_all | solution.py:42
  316.5 11.3 %copy.65 = bf16[4,1,2,1,128,8,512]{4,6,5,2,0,3,1:T(8,128)(2,1)} copy(bf16[4,1,2,1,128,8,512]{6,4,2,5,0,3,1:T(8,128)(2,1)} %bitcast.15) | data formatting | bytes 16777216 | tf_op jit(solution)/shard_map/transpose | solution.py:44
  327.8 12.0 %copy.66 = bf16[2,32,1,4,128,128]{5,4,3,1,0,2:T(8,128)(2,1)} copy(bf16[2,32,1,4,128,128]{4,5,1,0,3,2:T(8,128)(2,1)} %bitcast.88) | data formatting | bytes 16777216 | tf_op jit(solution)/shard_map/transpose | solution.py:64
  339.8 14.6 %gather_fusion.3 = bf16[192,512,128]{2,1,0:T(8,128)(2,1)} fusion(bf16[64,1,512,128]{3,2,0,1:T(8,128)(2,1)} %bitcast.83, s32[192]{0:T(256)S(1)} %reshape.181), kind=kCustom, calls=%fused_computation.3 | custom fusion | bytes 50333184 | tf_op jit(solution)/shard_map/gather | solution.py:73
  354.4 16.3 %bitcast_select_fusion = f32[48,512,128]{2,1,0:T(8,128)} fusion(pred[48]{0:T(512)(128)(4,1)S(1)} %iota_compare_fusion.1, bf16[48,4,512,128]{3,2,1,0:T(8,128)(2,1)} %bitcast.90, bf16[48,4,128,128]{3,2,1,0:T(8,128)(2,1)} %gather_fusion.4), kind=kOutput, calls=%fused_computation.17 | convolution fusion | flops 3224371200 | bytes 44040240 | tf_op jit(solution)/shard_map/emrc,emcb->erb/dot_general | solution.py:74
  370.7 7.8 %broadcast_in_dim.61 = f32[64,512,128]{2,1,0:T(8,128)} broadcast(f32[]{:T(128)} %constant.22.clone.1), dimensions={} | broadcast | bytes 16777220 | tf_op jit(solution)/shard_map/broadcast_in_dim | solution.py:79
  378.5 28.1 %scatter_fusion = f32[64,512,128]{2,1,0:T(8,128)} fusion(f32[64,512,128]{2,1,0:T(8,128)} %broadcast_in_dim.61, s32[48]{0:T(128)S(1)} %fusion.6, f32[48,512,128]{2,1,0:T(8,128)} %bitcast_select_fusion), kind=kCustom, calls=%fused_computation.5 | custom fusion | flops 3145728 | bytes 37748928 | tf_op jit(solution)/shard_map/scatter-add | solution.py:79
  406.6 9.2 %convert_element_type.31 = bf16[64,512,128]{2,1,0:T(8,128)(2,1)} convert(f32[64,512,128]{2,1,0:T(8,128)} %scatter_fusion) | non-fusion elementwise | flops 4194304 | bytes 25165824 | tf_op jit(solution)/shard_map/convert_element_type | solution.py:82
  415.7 12.0 %copy.68 = bf16[4,2,1,128,32,128]{3,5,4,1,0,2:T(8,128)(2,1)} copy(bf16[4,2,1,128,32,128]{5,3,0,4,1,2:T(8,128)(2,1)} %bitcast.84) | data formatting | bytes 16777216 | tf_op jit(solution)/shard_map/transpose | solution.py:85
  427.7 11.4 %copy.69 = bf16[4,8,1,2,1,128,512]{6,5,3,1,0,4,2:T(8,128)(2,1)} copy(bf16[4,8,1,2,1,128,512]{5,6,1,3,0,4,2:T(8,128)(2,1)} %bitcast.89) | data formatting | bytes 16777216 | tf_op jit(solution)/shard_map/transpose | solution.py:89
  439.1 9.2 %all-to-all-start.1 = ((bf16[32,1,2,1,1,128,512]{6,5,2,4,3,1,0:T(8,128)(2,1)}), bf16[32,1,2,1,1,128,512]{6,5,2,4,3,1,0:T(8,128)(2,1)}, u32[]{:S(2)}, u32[]{:S(2)}) async-start(bf16[32,1,2,1,1,128,512]{6,5,2,4,3,1,0:T(8,128)(2,1)} %bitcast.87), calls=%async_computation.1 | async-start | bytes 16777216 | tf_op jit(solution)/shard_map/all_to_all | solution.py:92
  448.3 0.1 reshape.147
  448.4 16.4 %copy.61 = bf16[4096,1,2,512]{3,2,0,1:T(2,128)(2,1)} copy(bf16[4096,1,2,512]{3,0,2,1:T(8,128)(2,1)} %bitcast.86) | data formatting | bytes 16777216 | tf_op jit(solution)/shard_map/transpose | solution.py:47
  464.7 14.3 %reshape.148 = bf16[32,128,1024]{2,1,0:T(8,128)(2,1)} reshape(bf16[4096,1,2,512]{3,2,0,1:T(2,128)(2,1)} %copy.61) | data formatting | bytes 16777216 | tf_op jit(solution)/shard_map/reshape | solution.py:47
  479.0 12.1 %copy.60 = bf16[1,2,4096,512]{2,3,1,0:T(8,128)(2,1)} copy(bf16[1,2,4096,512]{3,2,1,0:T(8,128)(2,1)} %param.16) | data formatting | bytes 16777216 | tf_op args[1]
  491.2 0.6 dynamic_slice.27
  491.9 1.2 select_reduce_fusion
  493.1 0.2 fusion.5
  493.3 5.0 add_subtract_fusion
  498.3 108.1 %while.10 = (s32[]{:T(128)}, f32[4,8,128,1024]{3,2,1,0:T(8,128)}, s32[4]{0:T(128)S(1)}, s32[32,8]{1,0:T(8,128)S(1)}, bf16[256,128,128]{2,1,0:T(8,128)(2,1)}, /*i...) while((s32[]{:T(128)}, f32[4,8,128,1024]{3,2,1,0:T(8,128)}, ...), condition=%wide.region_1.2_spmd, body=%wide.region_0.1_spmd.sunk | while | flops 2147486208 | bytes 60829860 | solution.py:61
  498.3 0.6 dynamic_slice.36
  500.6 0.1 reshape.220
  500.7 4.3 gather_fusion
  505.0 0.1 constant_dynamic-slice_fusion.2
  505.2 0.1 reshape.221
  505.3 11.0 %gather_fusion.1 = bf16[64,128,1024]{2,1,0:T(8,128)(2,1)} fusion(bf16[32,128,1024]{2,1,0:T(8,128)(2,1)} %get-tuple-element.168, s32[1024]{0:T(1024)S(1)} %pad_clamp_fusion.6), kind=kCustom, calls=%fused_computation.1.clone.1 | custom fusion | bytes 33554688 | tf_op jit(solution)/shard_map/while/body/eval_jaxpr/gather | solution.py:54
  516.2 9.0 %bitcast_dynamic-update-slice_fusion.2 = f32[4,8,128,1024]{3,2,1,0:T(8,128)} fusion(f32[4,8,128,1024]{3,2,1,0:T(8,128)} %get-tuple-element.153, s32[]{:T(128)S(6)} %copy.83, bf16[8,8,128,128]{3,2,1,0:T(8,128)(2,1)S(1)} %bitcast.82, bf16[8,8,128,1024]{3,2,1,0:T(8,128)(2,1)} %bitcast.81), kind=kOutput, calls=%fused_computation.6.clone.1 | convolution fusion | flops 2147483648 | bytes 23068676 | tf_op jit(solution)/shard_map/while/body/eval_jaxpr/akrc,akce->are/dot_general | solution.py:56
  525.2 0.6 dynamic_slice.36
  527.6 0.1 reshape.220
  527.7 4.3 gather_fusion
  532.2 0.1 reshape.221
  532.3 11.0 %gather_fusion.1 = bf16[64,128,1024]{2,1,0:T(8,128)(2,1)} fusion(bf16[32,128,1024]{2,1,0:T(8,128)(2,1)} %get-tuple-element.168, s32[1024]{0:T(1024)S(1)} %pad_clamp_fusion.6), kind=kCustom, calls=%fused_computation.1.clone.1 | custom fusion | bytes 33554688 | tf_op jit(solution)/shard_map/while/body/eval_jaxpr/gather | solution.py:54
  543.3 9.0 %bitcast_dynamic-update-slice_fusion.2 = f32[4,8,128,1024]{3,2,1,0:T(8,128)} fusion(f32[4,8,128,1024]{3,2,1,0:T(8,128)} %get-tuple-element.153, s32[]{:T(128)S(6)} %copy.83, bf16[8,8,128,128]{3,2,1,0:T(8,128)(2,1)S(1)} %bitcast.82, bf16[8,8,128,1024]{3,2,1,0:T(8,128)(2,1)} %bitcast.81), kind=kOutput, calls=%fused_computation.6.clone.1 | convolution fusion | flops 2147483648 | bytes 23068676 | tf_op jit(solution)/shard_map/while/body/eval_jaxpr/akrc,akce->are/dot_general | solution.py:56
  552.3 0.6 dynamic_slice.36
  554.6 0.1 reshape.220
  554.7 4.3 gather_fusion
  559.2 0.1 reshape.221
  559.3 11.0 %gather_fusion.1 = bf16[64,128,1024]{2,1,0:T(8,128)(2,1)} fusion(bf16[32,128,1024]{2,1,0:T(8,128)(2,1)} %get-tuple-element.168, s32[1024]{0:T(1024)S(1)} %pad_clamp_fusion.6), kind=kCustom, calls=%fused_computation.1.clone.1 | custom fusion | bytes 33554688 | tf_op jit(solution)/shard_map/while/body/eval_jaxpr/gather | solution.py:54
  570.3 9.0 %bitcast_dynamic-update-slice_fusion.2 = f32[4,8,128,1024]{3,2,1,0:T(8,128)} fusion(f32[4,8,128,1024]{3,2,1,0:T(8,128)} %get-tuple-element.153, s32[]{:T(128)S(6)} %copy.83, bf16[8,8,128,128]{3,2,1,0:T(8,128)(2,1)S(1)} %bitcast.82, bf16[8,8,128,1024]{3,2,1,0:T(8,128)(2,1)} %bitcast.81), kind=kOutput, calls=%fused_computation.6.clone.1 | convolution fusion | flops 2147483648 | bytes 23068676 | tf_op jit(solution)/shard_map/while/body/eval_jaxpr/akrc,akce->are/dot_general | solution.py:56
  579.3 0.6 dynamic_slice.36
  581.7 0.1 reshape.220
  581.8 4.3 gather_fusion
  586.3 0.1 reshape.221
  586.3 11.0 %gather_fusion.1 = bf16[64,128,1024]{2,1,0:T(8,128)(2,1)} fusion(bf16[32,128,1024]{2,1,0:T(8,128)(2,1)} %get-tuple-element.168, s32[1024]{0:T(1024)S(1)} %pad_clamp_fusion.6), kind=kCustom, calls=%fused_computation.1.clone.1 | custom fusion | bytes 33554688 | tf_op jit(solution)/shard_map/while/body/eval_jaxpr/gather | solution.py:54
  597.3 9.0 %bitcast_dynamic-update-slice_fusion.2 = f32[4,8,128,1024]{3,2,1,0:T(8,128)} fusion(f32[4,8,128,1024]{3,2,1,0:T(8,128)} %get-tuple-element.153, s32[]{:T(128)S(6)} %copy.83, bf16[8,8,128,128]{3,2,1,0:T(8,128)(2,1)S(1)} %bitcast.82, bf16[8,8,128,1024]{3,2,1,0:T(8,128)(2,1)} %bitcast.81), kind=kOutput, calls=%fused_computation.6.clone.1 | convolution fusion | flops 2147483648 | bytes 23068676 | tf_op jit(solution)/shard_map/while/body/eval_jaxpr/akrc,akce->are/dot_general | solution.py:56
  606.3 22.0 %reshape.209 = f32[4096,1,2,512]{3,2,0,1:T(2,128)} reshape(f32[4,8,128,1024]{3,2,1,0:T(8,128)} %get-tuple-element.42) | data formatting | bytes 33554432 | tf_op jit(solution)/shard_map/reshape | solution.py:62
  628.3 25.0 %copy.75 = f32[4096,1,2,512]{0,3,2,1:T(8,128)} copy(f32[4096,1,2,512]{3,2,0,1:T(2,128)} %reshape.209) | data formatting | bytes 33554432 | tf_op jit(solution)/shard_map/reshape | solution.py:62
  653.3 11.5 %convert_bitcast_fusion = f32[1,1,2,1,32,1,128,512]{7,6,2,4,5,3,1,0:T(8,128)} fusion(bf16[32,1,2,1,1,128,512]{6,5,2,4,3,1,0:T(8,128)(2,1)} %all-to-all-done.1), kind=kLoop, calls=%fused_computation.12 | loop fusion | flops 4194304 | bytes 25165824 | tf_op jit(solution)/shard_map/convert_element_type | solution.py:110
  664.9 20.2 %copy.71 = f32[1,1,2,1,32,1,128,512]{6,4,7,2,5,3,1,0:T(8,128)} copy(f32[1,1,2,1,32,1,128,512]{7,6,2,4,5,3,1,0:T(8,128)} %convert_bitcast_fusion) | data formatting | bytes 33554432 | tf_op jit(solution)/shard_map/convert_element_type | solution.py:110
  685.1 18.2 %reshape.155 = f32[1,2,4096,512]{2,3,1,0:T(8,128)} reshape(f32[1,1,2,1,32,1,128,512]{6,4,7,2,5,3,1,0:T(8,128)} %copy.71) | data formatting | bytes 33554432 | tf_op jit(solution)/shard_map/convert_element_type | solution.py:110
  703.3 20.5 %fusion.2 = bf16[1,2,4096,512]{2,3,1,0:T(8,128)(2,1)} fusion(f32[1,2,4096,512]{2,3,1,0:T(8,128)} %reshape.155, f32[4096,1,2,512]{0,3,2,1:T(8,128)} %copy.75, bf16[1,2,4096,512]{2,3,1,0:T(8,128)(2,1)} %copy.60, f32[2]{0:T(128)S(1)} %fusion.5, f32[4096,512]{0,1:T(8,128)} %add_subtract_fusion), kind=kLoop, calls=%fused_computation.16 | loop fusion | flops 25165824 | bytes 58720264 | tf_op jit(solution)/shard_map/convert_element_type | solution.py:111
  723.9 11.9 %copy.72 = bf16[1,2,4096,512]{3,2,1,0:T(8,128)(2,1)} copy(bf16[1,2,4096,512]{2,3,1,0:T(8,128)(2,1)} %fusion.2) | data formatting | bytes 16777216 | tf_op jit(solution)/shard_map/convert_element_type | solution.py:111
  (48 shorter events, 0.8 us)
Async XLA Ops:
  6.5 267.8 %all-gather.5.cloned.1.call-start = ((), (), s32[]{:S(2)}) async-start(), calls=%async_computation.3 | async-start | bytes 9437184 | tf_op jit(solution)/shard_map/all_gather | solution.py:37
  15.0 6.8 copy-start.3
  15.0 6.9 copy-start.6
  15.0 301.5 %all-to-all-start = ((bf16[1,1,2,1,32,128,512]{6,5,2,3,1,0,4:T(8,128)(2,1)}), bf16[1,1,2,1,32,128,512]{6,5,2,3,1,0,4:T(8,128)(2,1)}, u32[]{:S(2)}, u32[]{:S(2)}) async-start(bf16[1,1,2,1,32,128,512]{6,5,2,3,1,0,4:T(8,128)(2,1)} %copy.64), calls=%async_computation | async-start | bytes 16777216 | tf_op jit(solution)/shard_map/all_to_all | solution.py:42
  21.1 477.2 %all-gather.3.cloned.1.call-start = ((), (), s32[]{:S(2)}) async-start(), calls=%async_computation.2 | async-start | bytes 9437184 | tf_op jit(solution)/shard_map/all_gather | solution.py:36
  439.1 9.2 %copy-start.4 = (s32[256]{0:T(256)S(1)}, s32[256]{0:T(256)}, u32[]{:S(2)}) copy-start(s32[256]{0:T(256)} %param.20) | copy-start | bytes 3076
  439.1 214.3 %all-to-all-start.1 = ((bf16[32,1,2,1,1,128,512]{6,5,2,4,3,1,0:T(8,128)(2,1)}), bf16[32,1,2,1,1,128,512]{6,5,2,4,3,1,0:T(8,128)(2,1)}, u32[]{:S(2)}, u32[]{:S(2)}) async-start(bf16[32,1,2,1,1,128,512]{6,5,2,4,3,1,0:T(8,128)(2,1)} %bitcast.87), calls=%async_computation.1 | async-start | bytes 16777216 | tf_op jit(solution)/shard_map/all_to_all | solution.py:92
  479.0 12.1 %copy-start.7 = (s32[4]{0:T(128)S(1)}, s32[4]{0:T(128)}, u32[]{:S(2)}) copy-start(s32[4]{0:T(128)} %param.24) | copy-start | bytes 52
  479.0 12.8 %copy-start.1 = (f32[4096]{0:T(1024)S(1)}, f32[4096]{0:T(1024)}, u32[]{:S(2)}) copy-start(f32[4096]{0:T(1024)} %param.27) | copy-start | bytes 49156
  479.0 12.8 %copy-start.2 = (f32[400]{0:T(512)S(1)}, f32[400]{0:T(512)}, u32[]{:S(2)}) copy-start(f32[400]{0:T(512)} %param.26) | copy-start | bytes 4804
  479.0 14.1 %copy-start.5 = (s32[2]{0:T(128)S(1)}, s32[2]{0:T(128)}, u32[]{:S(2)}) copy-start(s32[2]{0:T(128)} %param.25) | copy-start | bytes 28
  479.0 19.2 %copy-start = (s32[32,8]{0,1:T(8,128)S(1)}, s32[32,8]{0,1:T(8,128)}, u32[]{:S(2)}) copy-start(s32[32,8]{0,1:T(8,128)} %param.19) | copy-start | bytes 3076
Sparse Core Ops, SparseCore 0:
  9.5 264.8 all-gather.4
  276.5 137.1 all-gather.2
where the time goes:
time: 749 us; the launch traced here: 743 us
  local copies, waits for them, and re-layouts  292 us (39%)
  waiting for transfers between devices  285 us (38%)
  other arithmetic  77.2 us (10%)
  matrix products  52.4 us (7%)
  starting transfers between devices  15.2 us (2%)
  between operations  13.5 us (2%)
    all_gather x1, waiting for transfers between devices, body(): lax.all_gather(cycle_tiles, 'vir', axis=0, tiled=True)  250 us
    reshape x2, local copies, waits for them, and re-layouts, body(): total.reshape(width_all, slab_rows, window, block_cols)  47 us
    gather x4, local copies, waits for them, and re-layouts, ladder_block(): picked_rows = arranged[screen_part]  43.9 us
    convert_element_type x2, local copies, waits for them, and re-layouts, body(): value = coulomb.astype(jnp.float32) + ladder + cycle.astype(jnp.float32)  38.4 us
    dot_general x4, matrix products, ladder_block(): jnp.einsum('akrc,akce->are', weights, picked_rows, preferred_element_type...  36.1 us
    all_to_all x1, waiting for transfers between devices, body(): lax.all_to_all(flat, ('occ', 'vir'), split_axis=4, concat_axis=0, tiled=T...  33.9 us
    scatter-add x1, other arithmetic, body(): jnp.zeros((column_tiles, slab_all * inner, tile_side), jnp.float32)  28.1 us
    convert_element_type x1, other arithmetic, body(): return (value / denominator).astype(jnp.bfloat16)  20.5 us
  transfers between devices with their start and end apart: 4, of which 2 were waited for; matrix products, arithmetic and copies ran while one was open for 46% of the time, Pallas kernels for 0%

commit v1 on v0

v1 whole, which is shorter than its diff:
```python
import functools

import jax
import jax.numpy as jnp
from jax import lax
from jax.experimental import pallas as pl
from jax.experimental.pallas import tpu as pltpu
from jax.sharding import PartitionSpec as P

MESH = pl.DeviceIdType.MESH
VMEM_BYTES = 56 * 1024 * 1024


def bits_down(count):
    bits, bit = [], count // 2
    while bit >= 1:
        bits.append(bit)
        bit //= 2
    return bits


def flipped(index, bit):
    return index + bit - 2 * bit * ((index // bit) % 2)


def spread_order(count):
    return sorted(range(1, count), key=lambda step: abs(step - count // 2))


def send_kernel(occ_count, vir_count, t_ref, w_ref, z_ref, tx_ref, wall_ref, zall_ref,
                own_sem, t_send, t_recv, g_send, g_recv):
    occ, vir = lax.axis_index("occ"), lax.axis_index("vir")
    rows = tx_ref.shape[2]
    sub = wall_ref.shape[2]
    occ_bits, vir_bits = bits_down(occ_count), bits_down(vir_count)

    barrier = pltpu.get_barrier_semaphore()
    for step in range(1, vir_count):
        peer = (vir + step) % vir_count
        pl.semaphore_signal(barrier, inc=1, device_id=(occ, peer), device_id_type=MESH)
    for bit in occ_bits:
        pl.semaphore_signal(barrier, inc=1, device_id=(flipped(occ, bit), vir), device_id_type=MESH)
    pl.semaphore_wait(barrier, vir_count - 1 + len(occ_bits))

    own = []
    for place, (src, dst) in enumerate(((w_ref, wall_ref), (z_ref, zall_ref))):
        copy = pltpu.make_async_copy(src.at[pl.ds(occ * sub, sub)], dst.at[vir, occ], own_sem.at[place])
        copy.start()
        own.append(copy)
    keep = pltpu.make_async_copy(t_ref.at[0, :, pl.ds(vir * rows, rows), :], tx_ref.at[vir], own_sem.at[2])
    keep.start()
    for copy in own:
        copy.wait()

    count = 0

    def exchange(views, device_id):
        nonlocal count
        copies = []
        for view in views:
            for ref in (zall_ref, wall_ref):
                copy = pltpu.make_async_remote_copy(
                    src_ref=view(ref), dst_ref=view(ref), send_sem=g_send.at[count], recv_sem=g_recv.at[count],
                    device_id=device_id, device_id_type=MESH)
                copy.start()
                copies.append(copy)
                count += 1
        return copies

    bit = vir_bits[0]
    pending = exchange([lambda ref: ref.at[vir, occ]], (occ, flipped(vir, bit)))
    held = [vir, flipped(vir, bit)]

    moves = []
    for place, step in enumerate(spread_order(vir_count)):
        peer = (vir + step) % vir_count
        copy = pltpu.make_async_remote_copy(
            src_ref=t_ref.at[0, :, pl.ds(peer * rows, rows), :], dst_ref=tx_ref.at[vir],
            send_sem=t_send.at[place], recv_sem=t_recv.at[place],
            device_id=(occ, peer), device_id_type=MESH)
        copy.start()
        moves.append(copy)

    for copy in pending:
        copy.wait()
    for bit in vir_bits[1:]:
        pending = exchange([functools.partial(lambda at, ref: ref.at[at, occ], at) for at in held],
                           (occ, flipped(vir, bit)))
        for copy in pending:
            copy.wait()
        held = held + [flipped(at, bit) for at in held]
    held = [occ]
    for bit in occ_bits:
        pending = exchange([functools.partial(lambda at, ref: ref.at[:, at], at) for at in held],
                           (flipped(occ, bit), vir))
        for copy in pending:
            copy.wait()
        held = held + [flipped(at, bit) for at in held]
    keep.wait()
    for copy in moves:
        copy.wait()


def send_tiles(amplitudes, ladder_tiles, cycle_tiles, occ_count, vir_count):
    slab_rows, window, width_all, block_cols = amplitudes.shape
    stored, side, _ = ladder_tiles.shape
    rows, sub = width_all // vir_count, stored // occ_count
    gathers = 2 * (vir_count - 1 + occ_count - 1)
    every = jax.ShapeDtypeStruct((vir_count, occ_count, sub, side, side), jnp.bfloat16)
    return pl.pallas_call(
        functools.partial(send_kernel, occ_count, vir_count),
        out_shape=(jax.ShapeDtypeStruct((vir_count, window, rows, block_cols), jnp.bfloat16), every, every),
        in_specs=[pl.BlockSpec(memory_space=pl.ANY)] * 3,
        out_specs=(pl.BlockSpec(memory_space=pl.ANY),) * 3,
        scratch_shapes=[
            pltpu.SemaphoreType.DMA((3,)),
            pltpu.SemaphoreType.DMA((vir_count - 1,)),
            pltpu.SemaphoreType.DMA((vir_count - 1,)),
            pltpu.SemaphoreType.DMA((gathers,)),
            pltpu.SemaphoreType.DMA((gathers,)),
        ],
        compiler_params=pltpu.CompilerParams(
            collective_id=0, has_side_effects=True, vmem_limit_bytes=VMEM_BYTES),
    )(amplitudes, ladder_tiles, cycle_tiles)


def cycle_kernel(screen_ref, used_ref, tx_ref, z_ref, out_ref):
    vir_count, window, rows, block_cols = tx_ref.shape
    side = z_ref.shape[1]
    here, tiles_here = block_cols // side, rows // side
    keep = screen_ref.shape[1]
    tile_count = screen_ref.shape[0] // window
    dest = pl.program_id(0)
    for j in range(window):
        for col in range(here):
            q = j * tile_count + dest * here + col
            picked, weights = [], []
            for m in range(keep):
                u = screen_ref[q, m]
                k, tile = u // tile_count, u % tile_count
                lanes = pl.ds(pl.multiple_of((tile % here) * side, side), side)
                picked.append(tx_ref[tile // here, k, :, lanes])
                weights.append(z_ref[q * keep + m])
            part = jnp.dot(
                jnp.concatenate(picked, axis=1), jnp.concatenate(weights, axis=0),
                preferred_element_type=jnp.float32)
            for a in range(tiles_here):
                span = slice(a * side, (a + 1) * side)
                kept = jnp.where(used_ref[a, q] > 0, part[span], 0.0)
                out_ref[0, j, span, col * side:(col + 1) * side] = kept.astype(jnp.bfloat16)


def cycle_term(cycle_screen, used, moved, all_cycle):
    vir_count, window, rows, block_cols = moved.shape
    return pl.pallas_call(
        cycle_kernel,
        out_shape=jax.ShapeDtypeStruct(moved.shape, jnp.bfloat16),
        grid=(vir_count,),
        in_specs=[
            pl.BlockSpec(memory_space=pltpu.SMEM),
            pl.BlockSpec(memory_space=pltpu.SMEM),
            pl.BlockSpec(moved.shape, lambda d: (0, 0, 0, 0)),
            pl.BlockSpec(all_cycle.shape, lambda d: (0, 0, 0)),
        ],
        out_specs=pl.BlockSpec((1, window, rows, block_cols), lambda d: (d, 0, 0, 0)),
        compiler_params=pltpu.CompilerParams(vmem_limit_bytes=VMEM_BYTES),
    )(cycle_screen, used, moved, all_cycle)


def back_kernel(vir_count, part_ref, out_ref, own_sem, send_sem, recv_sem):
    occ, vir = lax.axis_index("occ"), lax.axis_index("vir")
    rows = part_ref.shape[2]
    barrier = pltpu.get_barrier_semaphore()
    for step in range(1, vir_count):
        peer = (vir + step) % vir_count
        pl.semaphore_signal(barrier, inc=1, device_id=(occ, peer), device_id_type=MESH)
    pl.semaphore_wait(barrier, vir_count - 1)
    place_here = out_ref.at[:, pl.ds(vir * rows, rows), :]
    moves = []
    for place, step in enumerate(spread_order(vir_count)):
        peer = (vir + step) % vir_count
        copy = pltpu.make_async_remote_copy(
            src_ref=part_ref.at[peer], dst_ref=place_here,
            send_sem=send_sem.at[place], recv_sem=recv_sem.at[place],
            device_id=(occ, peer), device_id_type=MESH)
        copy.start()
        moves.append(copy)
    keep = pltpu.make_async_copy(part_ref.at[vir], place_here, own_sem)
    keep.start()
    keep.wait()
    for copy in moves:
        copy.wait()


def send_back(part, vir_count):
    _, window, rows, block_cols = part.shape
    return pl.pallas_call(
        functools.partial(back_kernel, vir_count),
        out_shape=jax.ShapeDtypeStruct((window, vir_count * rows, block_cols), jnp.bfloat16),
        in_specs=[pl.BlockSpec(memory_space=pl.ANY)],
        out_specs=pl.BlockSpec(memory_space=pl.ANY),
        scratch_shapes=[
            pltpu.SemaphoreType.DMA,
            pltpu.SemaphoreType.DMA((vir_count - 1,)),
            pltpu.SemaphoreType.DMA((vir_count - 1,)),
        ],
        compiler_params=pltpu.CompilerParams(
            collective_id=1, has_side_effects=True, vmem_limit_bytes=VMEM_BYTES),
    )(part)


def update_kernel(screen_ref, slot_ref, energy_ref, t_ref, w_ref, row_ref, col_ref, near_ref, cycle_ref, out_ref):
    window = t_ref.shape[1]
    keep = screen_ref.shape[1]
    a = pl.program_id(0)
    weights = jnp.concatenate([w_ref[slot_ref[a * keep + k]] for k in range(keep)], axis=1)
    sums = row_ref[...] + col_ref[...] - energy_ref[0]
    for j in range(window):
        picked = jnp.concatenate([t_ref[0, j, screen_ref[a, k]] for k in range(keep)], axis=0)
        ladder = jnp.dot(weights, picked, preferred_element_type=jnp.float32)
        value = near_ref[0, j].astype(jnp.float32) + ladder + cycle_ref[j].astype(jnp.float32)
        out_ref[0, j] = (value / (sums - energy_ref[1 + j])).astype(jnp.bfloat16)


def update(ladder_screen, tile_slot, energies, amplitudes, all_ladder, energy_a, energy_b, coulomb, cycle):
    _, window, width_all, block_cols = amplitudes.shape
    side = all_ladder.shape[1]
    tile_count = width_all // side
    tiled = amplitudes.reshape(1, window, tile_count, side, block_cols)
    block = pl.BlockSpec((1, window, side, block_cols), lambda a: (0, 0, a, 0))
    smem = pl.BlockSpec(memory_space=pltpu.SMEM)
    return pl.pallas_call(
        update_kernel,
        out_shape=jax.ShapeDtypeStruct(amplitudes.shape, jnp.bfloat16),
        grid=(tile_count,),
        in_specs=[
            smem, smem, smem,
            pl.BlockSpec(tiled.shape, lambda a: (0, 0, 0, 0, 0)),
            pl.BlockSpec(all_ladder.shape, lambda a: (0, 0, 0)),
            pl.BlockSpec((side, 1), lambda a: (a, 0)),
            pl.BlockSpec((1, block_cols), lambda a: (0, 0)),
            block,
            pl.BlockSpec((window, side, block_cols), lambda a: (0, a, 0)),
        ],
        out_specs=block,
        compiler_params=pltpu.CompilerParams(vmem_limit_bytes=VMEM_BYTES),
    )(ladder_screen, tile_slot, energies, tiled, all_ladder, energy_a, energy_b, coulomb, cycle)


def body(
    amplitudes, coulomb, ladder_tiles, cycle_tiles, ladder_screen, tile_slot, cycle_screen,
    cycle_rows, cycle_count, slab_occ, window_occ, occ_energy, vir_energy,
):
    occ_count, vir_count = lax.axis_size("occ"), lax.axis_size("vir")
    slab_rows, window, width_all, block_cols = amplitudes.shape
    stored, side, _ = ladder_tiles.shape
    tile_count = width_all // side
    tiles_here = tile_count // vir_count
    occ, vir = lax.axis_index("occ"), lax.axis_index("vir")

    columns = lax.dynamic_slice_in_dim(cycle_rows, vir * tiles_here, tiles_here, 0)
    counts = lax.dynamic_slice_in_dim(cycle_count, vir * tiles_here, tiles_here, 0)
    listed = jnp.arange(columns.shape[1], dtype=jnp.int32)[None, :] < counts[:, None]
    every_q = jnp.arange(cycle_screen.shape[0], dtype=jnp.int32)
    used = jnp.any((columns[:, :, None] == every_q[None, None, :]) & listed[:, :, None], axis=1).astype(jnp.int32)

    orbital_ids = jnp.arange(occ_energy.shape[0], dtype=jnp.int32)
    wanted = jnp.concatenate([lax.dynamic_slice_in_dim(slab_occ, occ * slab_rows, slab_rows), window_occ])
    energies = jnp.sum(jnp.where(wanted[:, None] == orbital_ids[None, :], occ_energy[None, :], 0.0), axis=1)
    energy_a = vir_energy.reshape(width_all, 1)
    energy_b = lax.dynamic_slice_in_dim(vir_energy, vir * block_cols, block_cols).reshape(1, block_cols)

    moved, all_ladder, all_cycle = send_tiles(amplitudes, ladder_tiles, cycle_tiles, occ_count, vir_count)
    all_ladder = all_ladder.reshape(vir_count * stored, side, side)
    all_cycle = all_cycle.reshape(vir_count * stored, side, side)
    part = cycle_term(cycle_screen, used, moved, all_cycle)
    cycle = send_back(part, vir_count)
    return update(ladder_screen, tile_slot, energies, amplitudes, all_ladder, energy_a, energy_b, coulomb, cycle)


def solution(mesh):
    return jax.shard_map(
        body,
        mesh=mesh,
        in_specs=(
            P("occ", None, None, "vir"),
            P("occ", None, None, "vir"),
            P("vir", None, None),
            P("vir", None, None),
            P(), P(), P(), P(), P(), P(), P(), P(), P(),
        ),
        out_specs=P("occ", None, None, "vir"),
        check_vma=False,
    )
```

time: 749 us -> 619 us (0.83)
  Pallas kernels: 0 us -> 607 us
  local copies, waits for them, and re-layouts: 292 us -> 6.06 us
  waiting for transfers between devices: 285 us -> 0 us
  other arithmetic: 77.2 us -> 2.3 us
  matrix products: 52.4 us -> 0 us
  starting transfers between devices: 15.2 us -> 0 us
  between operations: 13.5 us -> 0.07 us
    pallas_call x0 -> x4, Pallas kernels: none -> 607 us  [the longest x1 363 us: send_tiles(): pl.pallas_call(functools.partial(send_kernel, occ_count, vir_count), out_...]
    all_gather x2 -> x0, waiting for transfers between devices: 250 us -> none  [the longest x1 250 us: body(): lax.all_gather(cycle_tiles, 'vir', axis=0, tiled=True)]
    gather x11 -> x0, local copies, waits for them, and re-layouts: 84.7 us -> none  [the longest x4 43.9 us: ladder_block(): picked_rows = arranged[screen_part]]
    transpose x5 -> x0, local copies, waits for them, and re-layouts: 63 us -> none  [the longest x1 16.4 us: body(): amplitudes.transpose(2, 0, 1, 3).reshape(tile_count, tile_side, extent)]
    reshape x4 -> x1, local copies, waits for them, and re-layouts: 61.4 us -> 1.98 us  [body(): energy_a = vir_energy.reshape(width_all, 1)]
    dot_general x5 -> x0, matrix products: 52.4 us -> none  [the longest x4 36.1 us: ladder_block(): jnp.einsum('akrc,akce->are', weights, picked_rows, preferred_element_type...]
    convert_element_type x3 -> x0, local copies, waits for them, and re-layouts: 50.4 us -> none  [the longest x2 38.4 us: body(): value = coulomb.astype(jnp.float32) + ladder + cycle.astype(jnp.float32)]
    convert_element_type x3 -> x1, other arithmetic: 41.2 us -> 0.6 us  [body(): jnp.any((columns[:, :, None] == every_q[None, None, :]) & listed[:, :, No...]
  transfers between devices with their start and end apart: 4 -> 0, of which waited for: 2 -> 0; matrix products, arithmetic and copies ran while one was open for 46% -> 0% of each run, Pallas kernels for 0% -> 0%
where the time goes in v1:
time: 619 us; the launch traced here: 616 us
  Pallas kernels  607 us (98%)
    pallas_call x1, Pallas kernels, send_tiles(): pl.pallas_call(functools.partial(send_kernel, occ_count, vir_count), out_...  363 us
    pallas_call x1, Pallas kernels, send_back(): pl.pallas_call(functools.partial(back_kernel, vir_count), out_shape=jax.S...  194 us
    pallas_call x1, Pallas kernels, update(): pl.pallas_call(update_kernel, out_shape=jax.ShapeDtypeStruct(amplitudes.s...  33.1 us
    pallas_call x1, Pallas kernels, cycle_term(): pl.pallas_call(cycle_kernel, out_shape=jax.ShapeDtypeStruct(moved.shape,...  17.3 us

profile of v1, /device:TPU:14, one launch (start us, length us, event | category | flops | bytes accessed | tf_op | source)
XLA Modules:
  0.0 615.9 jit_solution(77002214734234420)
XLA Ops:
  0.0 0.0 copy-start
  0.0 0.0 copy-start.4
  0.0 0.7 copy-done
  0.7 0.7 dynamic_slice.15
  1.5 0.1 iota_compare_fusion.2
  1.5 0.1 fusion.1
  1.7 0.6 convert_element_type.3.used_ref
  2.3 363.1 %shard_map.127 = (bf16[8,2,512,512]{3,2,1,0:T(8,128)(2,1)}, bf16[8,4,8,128,128]{4,3,2,1,0:T(8,128)(2,1)}, bf16[8,4,8,128,128]{4,3,2,1,0:T(8,128)(2,1)}) custom-call(bf16[1,2,4096,512]{3,2,1,0:T(8,128)(2,1)} %t_ref.1, bf16[32,128,128]{2,1,0:T(8,128)(2,1)} %w_ref.1, bf16[32,128,128]{2,1,0:T(8,128)(2,1)} %z_ref.1), custom_call_target="tpu_custom_call" | custom-call | tf_op jit(solution)/shard_map/pallas_call | solution.py:110
  365.4 0.0 copy-done.4
  365.4 0.7 copy.19.screen_ref
  366.1 17.3 %shard_map.128.part_ref = bf16[8,2,512,512]{3,2,1,0:T(8,128)(2,1)} custom-call(s32[64,4]{1,0:T(8,128)} %copy.19.screen_ref, s32[4,64]{1,0:T(4,128)} %convert_element_type.3.used_ref, bf16[8,2,512,512]{3,2,1,0:T(8,128)(2,1)} %get-tuple-element.9.tx_ref, bf16[256,128,128]{2,1,0:T(8,128)(2,1)} %bitcast.7), custom_call_target="tpu_custom_call" | custom-call | tf_op jit(solution)/shard_map/pallas_call | solution.py:155
  383.3 0.0 copy-start.2
  383.3 0.0 copy-start.6
  383.3 0.0 copy-start.7
  383.4 0.0 copy-start.5
  383.4 0.0 copy-start.3
  383.4 194.0 %shard_map.129.cycle_ref = bf16[2,4096,512]{2,1,0:T(8,128)(2,1)} custom-call(bf16[8,2,512,512]{3,2,1,0:T(8,128)(2,1)} %shard_map.128.part_ref), custom_call_target="tpu_custom_call" | custom-call | tf_op jit(solution)/shard_map/pallas_call | solution.py:197
  577.4 0.0 copy-done.2
  577.4 0.7 dynamic_slice.13
  578.1 0.0 copy-done.6
  578.1 0.6 dynamic_slice.12
  578.6 0.0 copy-done.7
  578.7 0.7 pad_add_fusion
  579.4 0.0 copy-done.5
  579.4 0.8 select_reduce_fusion.energy_ref
  580.2 2.0 copy.21.row_ref
  582.1 0.0 copy-done.3
  582.1 0.7 copy.20.screen_ref
  582.8 0.0 copy-start.1
  582.8 33.1 %shard_map.130 = bf16[1,2,4096,512]{3,2,1,0:T(8,128)(2,1)} custom-call(s32[32,8]{1,0:T(8,128)} %copy.20.screen_ref, s32[256]{0:T(256)} %slot_ref.1, f32[3]{0:T(128)} %select_reduce_fusion.energy_ref, bf16[1,2,32,128,512]{4,3,2,1,0:T(8,128)(2,1)} %bitcast.5, bf16[256,128,128]{2,1,0:T(8,128)(2,1)} %bitcast.6, f32[4096,1]{1,0:T(8,128)} %copy.21.row_ref, ...), custom_call_target="tpu_custom_call" | custom-call | tf_op jit(solution)/shard_map/pallas_call | solution.py:232
  615.9 0.0 copy-done.1
  (1 shorter events, 0.0 us)
Async XLA Ops:
  0.0 0.7 copy-start
  0.0 365.4 %copy-start.4 = (s32[64,4]{0,1:T(4,128)S(1)}, s32[64,4]{0,1:T(4,128)}, u32[]{:S(2)}) copy-start(s32[64,4]{0,1:T(4,128)} %param.19) | copy-start | bytes 3076
  383.3 194.1 %copy-start.2 = (f32[4096]{0:T(1024)S(1)}, f32[4096]{0:T(1024)}, u32[]{:S(2)}) copy-start(f32[4096]{0:T(1024)} %param.25) | copy-start | bytes 49156
  383.3 194.7 %copy-start.6 = (s32[4]{0:T(128)S(1)}, s32[4]{0:T(128)}, u32[]{:S(2)}) copy-start(s32[4]{0:T(128)} %param.22) | copy-start | bytes 52
  383.3 195.3 %copy-start.7 = (s32[2]{0:T(128)S(1)}, s32[2]{0:T(128)}, u32[]{:S(2)}) copy-start(s32[2]{0:T(128)} %param.23) | copy-start | bytes 28
  383.4 196.0 %copy-start.5 = (f32[400]{0:T(512)S(1)}, f32[400]{0:T(512)}, u32[]{:S(2)}) copy-start(f32[400]{0:T(512)} %param.24) | copy-start | bytes 4804
  383.4 198.8 %copy-start.3 = (s32[32,8]{0,1:T(8,128)S(1)}, s32[32,8]{0,1:T(8,128)}, u32[]{:S(2)}) copy-start(s32[32,8]{0,1:T(8,128)} %param.17) | copy-start | bytes 3076
  582.8 33.1 %copy-start.1 = (s32[32,48]{1,0:T(8,128)S(1)}, s32[32,48]{1,0:T(8,128)}, u32[]{:S(2)}) copy-start(s32[32,48]{1,0:T(8,128)} %param.20) | copy-start | bytes 18436

commit v2 on v1

v2 whole, which is shorter than its diff:
```python
import functools

import jax
import jax.numpy as jnp
from jax import lax
from jax.experimental import pallas as pl
from jax.experimental.pallas import tpu as pltpu
from jax.sharding import PartitionSpec as P

MESH = pl.DeviceIdType.MESH
VMEM_BYTES = 56 * 1024 * 1024


def bits_down(count):
    bits, bit = [], count // 2
    while bit >= 1:
        bits.append(bit)
        bit //= 2
    return bits


def flipped(index, bit):
    return index + bit - 2 * bit * ((index // bit) % 2)


def spread_order(count):
    return sorted(range(1, count), key=lambda step: abs(step - count // 2))


def gather_stages(ref, occ, vir, occ_count, vir_count, send_sem, recv_sem):
    def copies(views, device_id, first):
        return [
            pltpu.make_async_remote_copy(
                src_ref=view, dst_ref=view, send_sem=send_sem.at[first + at], recv_sem=recv_sem.at[first + at],
                device_id=device_id, device_id_type=MESH)
            for at, view in enumerate(views)
        ]

    stages, first = [], 0
    held = [vir]
    for bit in bits_down(vir_count):
        stages.append(copies([ref.at[at, occ] for at in held], (occ, flipped(vir, bit)), first))
        first += len(held)
        held = held + [flipped(at, bit) for at in held]
    held = [occ]
    for bit in bits_down(occ_count):
        stages.append(copies([ref.at[:, at] for at in held], (flipped(occ, bit), vir), first))
        first += len(held)
        held = held + [flipped(at, bit) for at in held]
    return stages


def exchange_kernel(occ_count, vir_count, outward, many_ref, tile_ref, out_ref, every_ref,
                    own_sem, m_send, m_recv, g_send, g_recv):
    occ, vir = lax.axis_index("occ"), lax.axis_index("vir")
    sub, side = every_ref.shape[2], every_ref.shape[3]
    window = out_ref.shape[1 if outward else 0]
    rows = out_ref.shape[2] if outward else many_ref.shape[2]

    barrier = pltpu.get_barrier_semaphore()
    for step in range(1, vir_count):
        peer = (vir + step) % vir_count
        pl.semaphore_signal(barrier, inc=1, device_id=(occ, peer), device_id_type=MESH)
    for bit in bits_down(occ_count):
        pl.semaphore_signal(barrier, inc=1, device_id=(flipped(occ, bit), vir), device_id_type=MESH)

    mine = pltpu.make_async_copy(tile_ref.at[pl.ds(occ * sub, sub)], every_ref.at[vir, occ], own_sem.at[0])
    mine.start()

    def source(peer, j, start):
        if outward:
            return many_ref.at[0, j, pl.ds(peer * rows + start, side), :]
        return many_ref.at[peer, j, pl.ds(start, side), :]

    def target(j, start):
        if outward:
            return out_ref.at[vir, j, pl.ds(start, side), :]
        return out_ref.at[j, pl.ds(vir * rows + start, side), :]

    chunks = [(j, start) for start in range(0, rows, side) for j in range(window)]
    keeps = [
        pltpu.make_async_copy(source(vir, j, start), target(j, start), own_sem.at[1 + at])
        for at, (j, start) in enumerate(chunks)
    ]
    order = spread_order(vir_count)
    moves = []

    def move_next():
        if len(moves) == len(chunks) * len(order):
            return
        j, start = chunks[len(moves) // len(order)]
        for step in order:
            peer, at = (vir + step) % vir_count, len(moves)
            copy = pltpu.make_async_remote_copy(
                src_ref=source(peer, j, start), dst_ref=target(j, start),
                send_sem=m_send.at[at], recv_sem=m_recv.at[at],
                device_id=(occ, peer), device_id_type=MESH)
            copy.start()
            moves.append(copy)

    mine.wait()
    pl.semaphore_wait(barrier, vir_count - 1 + len(bits_down(occ_count)))
    stages = gather_stages(every_ref, occ, vir, occ_count, vir_count, g_send, g_recv)
    wide = len(bits_down(vir_count))
    for at, stage in enumerate(stages):
        for copy in stage:
            copy.start()
        move_next()
        if at == 0:
            for copy in keeps:
                copy.start()
        if at >= wide:
            move_next()
        if at == len(stages) - 1:
            for _ in chunks:
                move_next()
        for copy in stage:
            copy.wait()
    for copy in keeps:
        copy.wait()
    for copy in moves:
        copy.wait()


def exchange(many, tiles, out_shape, occ_count, vir_count, outward):
    stored, side, _ = tiles.shape
    rows, window = (out_shape[2], out_shape[1]) if outward else (many.shape[2], many.shape[1])
    chunks = rows // side * window
    moves, gathers = chunks * (vir_count - 1), vir_count - 1 + occ_count - 1
    every = (vir_count, occ_count, stored // occ_count, side, side)
    out, gathered = pl.pallas_call(
        functools.partial(exchange_kernel, occ_count, vir_count, outward),
        out_shape=(jax.ShapeDtypeStruct(out_shape, jnp.bfloat16), jax.ShapeDtypeStruct(every, jnp.bfloat16)),
        in_specs=[pl.BlockSpec(memory_space=pl.ANY)] * 2,
        out_specs=(pl.BlockSpec(memory_space=pl.ANY),) * 2,
        scratch_shapes=[
            pltpu.SemaphoreType.DMA((1 + chunks,)),
            pltpu.SemaphoreType.DMA((moves,)),
            pltpu.SemaphoreType.DMA((moves,)),
            pltpu.SemaphoreType.DMA((gathers,)),
            pltpu.SemaphoreType.DMA((gathers,)),
        ],
        compiler_params=pltpu.CompilerParams(
            collective_id=0 if outward else 1, has_side_effects=True, vmem_limit_bytes=VMEM_BYTES),
    )(many, tiles)
    return out, gathered.reshape(vir_count * stored, side, side)


def cycle_kernel(screen_ref, used_ref, tx_ref, z_ref, out_ref):
    vir_count, window, rows, block_cols = tx_ref.shape
    side = z_ref.shape[1]
    here, tiles_here = block_cols // side, rows // side
    keep = screen_ref.shape[1]
    tile_count = screen_ref.shape[0] // window
    dest = pl.program_id(0)
    for j in range(window):
        for col in range(here):
            q = j * tile_count + dest * here + col
            picked, weights = [], []
            for m in range(keep):
                u = screen_ref[q, m]
                k, tile = u // tile_count, u % tile_count
                lanes = pl.ds(pl.multiple_of((tile % here) * side, side), side)
                picked.append(tx_ref[tile // here, k, :, lanes])
                weights.append(z_ref[q * keep + m])
            part = jnp.dot(
                jnp.concatenate(picked, axis=1), jnp.concatenate(weights, axis=0),
                preferred_element_type=jnp.float32)
            for a in range(tiles_here):
                span = slice(a * side, (a + 1) * side)
                kept = jnp.where(used_ref[a, q] > 0, part[span], 0.0)
                out_ref[0, j, span, col * side:(col + 1) * side] = kept.astype(jnp.bfloat16)


def cycle_term(cycle_screen, used, moved, all_cycle):
    vir_count, window, rows, block_cols = moved.shape
    return pl.pallas_call(
        cycle_kernel,
        out_shape=jax.ShapeDtypeStruct(moved.shape, jnp.bfloat16),
        grid=(vir_count,),
        in_specs=[
            pl.BlockSpec(memory_space=pltpu.SMEM),
            pl.BlockSpec(memory_space=pltpu.SMEM),
            pl.BlockSpec(moved.shape, lambda d: (0, 0, 0, 0)),
            pl.BlockSpec(all_cycle.shape, lambda d: (0, 0, 0)),
        ],
        out_specs=pl.BlockSpec((1, window, rows, block_cols), lambda d: (d, 0, 0, 0)),
        compiler_params=pltpu.CompilerParams(vmem_limit_bytes=VMEM_BYTES),
    )(cycle_screen, used, moved, all_cycle)


def update_kernel(screen_ref, slot_ref, energy_ref, t_ref, w_ref, row_ref, col_ref, near_ref, cycle_ref, out_ref):
    window = t_ref.shape[1]
    keep = screen_ref.shape[1]
    a = pl.program_id(0)
    weights = jnp.concatenate([w_ref[slot_ref[a * keep + k]] for k in range(keep)], axis=1)
    sums = row_ref[...] + col_ref[...] - energy_ref[0]
    for j in range(window):
        picked = jnp.concatenate([t_ref[0, j, screen_ref[a, k]] for k in range(keep)], axis=0)
        ladder = jnp.dot(weights, picked, preferred_element_type=jnp.float32)
        value = near_ref[0, j].astype(jnp.float32) + ladder + cycle_ref[j].astype(jnp.float32)
        out_ref[0, j] = (value / (sums - energy_ref[1 + j])).astype(jnp.bfloat16)


def update(ladder_screen, tile_slot, energies, amplitudes, all_ladder, energy_a, energy_b, coulomb, cycle):
    _, window, width_all, block_cols = amplitudes.shape
    side = all_ladder.shape[1]
    tile_count = width_all // side
    tiled = amplitudes.reshape(1, window, tile_count, side, block_cols)
    block = pl.BlockSpec((1, window, side, block_cols), lambda a: (0, 0, a, 0))
    smem = pl.BlockSpec(memory_space=pltpu.SMEM)
    return pl.pallas_call(
        update_kernel,
        out_shape=jax.ShapeDtypeStruct(amplitudes.shape, jnp.bfloat16),
        grid=(tile_count,),
        in_specs=[
            smem, smem, smem,
            pl.BlockSpec(tiled.shape, lambda a: (0, 0, 0, 0, 0)),
            pl.BlockSpec(all_ladder.shape, lambda a: (0, 0, 0)),
            pl.BlockSpec((side, 1), lambda a: (a, 0)),
            pl.BlockSpec((1, block_cols), lambda a: (0, 0)),
            block,
            pl.BlockSpec((window, side, block_cols), lambda a: (0, a, 0)),
        ],
        out_specs=block,
        compiler_params=pltpu.CompilerParams(vmem_limit_bytes=VMEM_BYTES),
    )(ladder_screen, tile_slot, energies, tiled, all_ladder, energy_a, energy_b, coulomb, cycle)


def body(
    amplitudes, coulomb, ladder_tiles, cycle_tiles, ladder_screen, tile_slot, cycle_screen,
    cycle_rows, cycle_count, slab_occ, window_occ, occ_energy, vir_energy,
):
    occ_count, vir_count = lax.axis_size("occ"), lax.axis_size("vir")
    slab_rows, window, width_all, block_cols = amplitudes.shape
    stored, side, _ = ladder_tiles.shape
    tile_count = width_all // side
    tiles_here = tile_count // vir_count
    occ, vir = lax.axis_index("occ"), lax.axis_index("vir")

    columns = lax.dynamic_slice_in_dim(cycle_rows, vir * tiles_here, tiles_here, 0)
    counts = lax.dynamic_slice_in_dim(cycle_count, vir * tiles_here, tiles_here, 0)
    listed = jnp.arange(columns.shape[1], dtype=jnp.int32)[None, :] < counts[:, None]
    every_q = jnp.arange(cycle_screen.shape[0], dtype=jnp.int32)
    used = jnp.any((columns[:, :, None] == every_q[None, None, :]) & listed[:, :, None], axis=1).astype(jnp.int32)

    orbital_ids = jnp.arange(occ_energy.shape[0], dtype=jnp.int32)
    wanted = jnp.concatenate([lax.dynamic_slice_in_dim(slab_occ, occ * slab_rows, slab_rows), window_occ])
    energies = jnp.sum(jnp.where(wanted[:, None] == orbital_ids[None, :], occ_energy[None, :], 0.0), axis=1)
    energy_a = vir_energy.reshape(width_all, 1)
    energy_b = lax.dynamic_slice_in_dim(vir_energy, vir * block_cols, block_cols).reshape(1, block_cols)

    moved_shape = (vir_count, window, width_all // vir_count, block_cols)
    moved, all_cycle = exchange(amplitudes, cycle_tiles, moved_shape, occ_count, vir_count, True)
    part = cycle_term(cycle_screen, used, moved, all_cycle)
    cycle, all_ladder = exchange(part, ladder_tiles, amplitudes.shape[1:], occ_count, vir_count, False)
    return update(ladder_screen, tile_slot, energies, amplitudes, all_ladder, energy_a, energy_b, coulomb, cycle)


def solution(mesh):
    return jax.shard_map(
        body,
        mesh=mesh,
        in_specs=(
            P("occ", None, None, "vir"),
            P("occ", None, None, "vir"),
            P("vir", None, None),
            P("vir", None, None),
            P(), P(), P(), P(), P(), P(), P(), P(), P(),
        ),
        out_specs=P("occ", None, None, "vir"),
        check_vma=False,
    )
```

time: 619 us -> 470 us (0.76)
  Pallas kernels: 607 us -> 461 us
    pallas_call x2, Pallas kernels: 557 us -> 410 us  [exchange(): pl.pallas_call(functools.partial(exchange_kernel, occ_count, vir_count, o...]
where the time goes in v2:
time: 470 us; the launch traced here: 469 us
  Pallas kernels  461 us (98%)
  local copies, waits for them, and re-layouts  6.08 us (1%)
    pallas_call x2, Pallas kernels, exchange(): pl.pallas_call(functools.partial(exchange_kernel, occ_count, vir_count, o...  410 us
    pallas_call x1, Pallas kernels, update(): pl.pallas_call(update_kernel, out_shape=jax.ShapeDtypeStruct(amplitudes.s...  33.1 us
    pallas_call x1, Pallas kernels, cycle_term(): pl.pallas_call(cycle_kernel, out_shape=jax.ShapeDtypeStruct(moved.shape,...  17.2 us

profile of v2, /device:TPU:14, one launch (start us, length us, event | category | flops | bytes accessed | tf_op | source)
XLA Modules:
  0.0 468.9 jit_solution(15800125389644948817)
XLA Ops:
  0.0 0.0 copy-start
  0.0 0.0 copy-start.4
  0.0 0.7 copy-done
  0.7 0.7 dynamic_slice.14
  1.5 0.1 iota_compare_fusion.2
  1.5 0.1 fusion.1
  1.7 0.6 convert_element_type.3.used_ref
  2.3 205.8 %shard_map.127 = (bf16[8,2,512,512]{3,2,1,0:T(8,128)(2,1)}, bf16[8,4,8,128,128]{4,3,2,1,0:T(8,128)(2,1)}) custom-call(bf16[1,2,4096,512]{3,2,1,0:T(8,128)(2,1)} %many_ref.1, bf16[32,128,128]{2,1,0:T(8,128)(2,1)} %tile_ref.2), custom_call_target="tpu_custom_call" | custom-call | tf_op jit(solution)/shard_map/pallas_call | solution.py:131
  208.1 0.0 copy-done.4
  208.1 0.7 copy.19.screen_ref
  208.8 17.2 %shard_map.128.many_ref = bf16[8,2,512,512]{3,2,1,0:T(8,128)(2,1)} custom-call(s32[64,4]{1,0:T(8,128)} %copy.19.screen_ref, s32[4,64]{1,0:T(4,128)} %convert_element_type.3.used_ref, bf16[8,2,512,512]{3,2,1,0:T(8,128)(2,1)} %get-tuple-element.9.tx_ref, bf16[256,128,128]{2,1,0:T(8,128)(2,1)} %bitcast.7), custom_call_target="tpu_custom_call" | custom-call | tf_op jit(solution)/shard_map/pallas_call | solution.py:177
  226.1 0.0 copy-start.2
  226.1 0.0 copy-start.6
  226.1 0.0 copy-start.7
  226.1 0.0 copy-start.5
  226.1 0.0 copy-start.3
  226.1 204.4 %shard_map.129 = (bf16[2,4096,512]{2,1,0:T(8,128)(2,1)}, bf16[8,4,8,128,128]{4,3,2,1,0:T(8,128)(2,1)}) custom-call(bf16[8,2,512,512]{3,2,1,0:T(8,128)(2,1)} %shard_map.128.many_ref, bf16[32,128,128]{2,1,0:T(8,128)(2,1)} %tile_ref.3), custom_call_target="tpu_custom_call" | custom-call | tf_op jit(solution)/shard_map/pallas_call | solution.py:131
  430.5 0.0 copy-done.2
  430.5 0.7 dynamic_slice.15
  431.2 0.0 copy-done.6
  431.2 0.6 dynamic_slice.12
  431.8 0.0 copy-done.7
  431.8 0.7 pad_add_fusion
  432.5 0.0 copy-done.5
  432.5 0.7 select_reduce_fusion.energy_ref
  433.2 2.0 copy.21.row_ref
  435.2 0.0 copy-done.3
  435.2 0.7 copy.20.screen_ref
  435.8 0.0 copy-start.1
  435.8 33.1 %shard_map.130 = bf16[1,2,4096,512]{3,2,1,0:T(8,128)(2,1)} custom-call(s32[32,8]{1,0:T(8,128)} %copy.20.screen_ref, s32[256]{0:T(256)} %slot_ref.1, f32[3]{0:T(128)} %select_reduce_fusion.energy_ref, bf16[1,2,32,128,512]{4,3,2,1,0:T(8,128)(2,1)} %bitcast.5, bf16[256,128,128]{2,1,0:T(8,128)(2,1)} %bitcast.6, f32[4096,1]{1,0:T(8,128)} %copy.21.row_ref, ...), custom_call_target="tpu_custom_call" | custom-call | tf_op jit(solution)/shard_map/pallas_call | solution.py:212
  468.9 0.0 copy-done.1
  (1 shorter events, 0.0 us)
Async XLA Ops:
  0.0 0.7 copy-start
  0.0 208.1 %copy-start.4 = (s32[64,4]{0,1:T(4,128)S(1)}, s32[64,4]{0,1:T(4,128)}, u32[]{:S(2)}) copy-start(s32[64,4]{0,1:T(4,128)} %param.19) | copy-start | bytes 3076
  226.1 204.5 %copy-start.2 = (f32[4096]{0:T(1024)S(1)}, f32[4096]{0:T(1024)}, u32[]{:S(2)}) copy-start(f32[4096]{0:T(1024)} %param.25) | copy-start | bytes 49156
  226.1 205.1 %copy-start.6 = (s32[4]{0:T(128)S(1)}, s32[4]{0:T(128)}, u32[]{:S(2)}) copy-start(s32[4]{0:T(128)} %param.22) | copy-start | bytes 52
  226.1 205.7 %copy-start.7 = (s32[2]{0:T(128)S(1)}, s32[2]{0:T(128)}, u32[]{:S(2)}) copy-start(s32[2]{0:T(128)} %param.23) | copy-start | bytes 28
  226.1 206.4 %copy-start.5 = (f32[400]{0:T(512)S(1)}, f32[400]{0:T(512)}, u32[]{:S(2)}) copy-start(f32[400]{0:T(512)} %param.24) | copy-start | bytes 4804
  226.1 209.1 %copy-start.3 = (s32[32,8]{0,1:T(8,128)S(1)}, s32[32,8]{0,1:T(8,128)}, u32[]{:S(2)}) copy-start(s32[32,8]{0,1:T(8,128)} %param.17) | copy-start | bytes 3076
  435.8 33.1 %copy-start.1 = (s32[32,48]{1,0:T(8,128)S(1)}, s32[32,48]{1,0:T(8,128)}, u32[]{:S(2)}) copy-start(s32[32,48]{1,0:T(8,128)} %param.20) | copy-start | bytes 18436

commit v3 on v2

v3 whole, which is shorter than its diff:
```python
import functools

import jax
import jax.numpy as jnp
from jax import lax
from jax.experimental import pallas as pl
from jax.experimental.pallas import tpu as pltpu
from jax.sharding import PartitionSpec as P

MESH = pl.DeviceIdType.MESH
VMEM_BYTES = 60 * 1024 * 1024


def bits_down(count):
    bits, bit = [], count // 2
    while bit >= 1:
        bits.append(bit)
        bit //= 2
    return bits


def flipped(index, bit):
    return index + bit - 2 * bit * ((index // bit) % 2)


def spread_order(count):
    return sorted(range(1, count), key=lambda step: abs(step - count // 2))


def gather_stages(ref, occ, vir, occ_count, vir_count, send_sem, recv_sem):
    def copies(views, device_id, first):
        return [
            pltpu.make_async_remote_copy(
                src_ref=view, dst_ref=view, send_sem=send_sem.at[first + at], recv_sem=recv_sem.at[first + at],
                device_id=device_id, device_id_type=MESH)
            for at, view in enumerate(views)
        ]

    stages, first = [], 0
    held = [vir]
    for bit in bits_down(vir_count):
        stages.append(copies([ref.at[at, occ] for at in held], (occ, flipped(vir, bit)), first))
        first += len(held)
        held = held + [flipped(at, bit) for at in held]
    held = [occ]
    for bit in bits_down(occ_count):
        stages.append(copies([ref.at[:, at] for at in held], (flipped(occ, bit), vir), first))
        first += len(held)
        held = held + [flipped(at, bit) for at in held]
    return stages


def main_kernel(occ_count, vir_count, lscreen_ref, slot_ref, cscreen_ref, mask_ref, t_ref, w_ref, z_ref,
                cycle_ref, ladder_ref, *scratch):
    groups = 2
    tx, part, scratch = scratch[:groups], scratch[groups:2 * groups], scratch[2 * groups:]
    wall, zall, t_own, lad, picks, own_sem, lad_sem, m_send, m_recv, b_send, b_recv, z_send, z_recv, w_send, w_recv = scratch
    occ, vir = lax.axis_index("occ"), lax.axis_index("vir")
    _, window, tile_count, side, block_cols = t_ref.shape
    sub = wall.shape[2]
    stored = sub * occ_count
    tiles_here, here = tile_count // vir_count, block_cols // side
    depth = tiles_here // groups
    ladder_keep, cycle_keep = lscreen_ref.shape[1], cscreen_ref.shape[1]
    occ_bits = bits_down(occ_count)

    barrier = pltpu.get_barrier_semaphore()
    for step in range(1, vir_count):
        peer = (vir + step) % vir_count
        pl.semaphore_signal(barrier, inc=1, device_id=(occ, peer), device_id_type=MESH)
    for bit in occ_bits:
        pl.semaphore_signal(barrier, inc=1, device_id=(flipped(occ, bit), vir), device_id_type=MESH)

    mine = []
    for at, (src, dst) in enumerate(((z_ref, zall), (w_ref, wall))):
        copy = pltpu.make_async_copy(src.at[pl.ds(occ * sub, sub)], dst.at[vir, occ], own_sem.at[at])
        copy.start()
        mine.append(copy)
    whole = pltpu.make_async_copy(t_ref.at[0], t_own, own_sem.at[2])
    keeps = []

    def keep(src, dst):
        copy = pltpu.make_async_copy(src, dst, own_sem.at[3 + len(keeps)])
        copy.start()
        keeps.append(copy)
        return copy

    order = spread_order(vir_count)
    chunks = [(g, d, j) for g in range(groups) for d in range(depth) for j in range(window)]
    moves = [[] for _ in range(groups)]
    moved = 0

    def move_next():
        nonlocal moved
        if moved == len(chunks):
            return
        g, d, j = chunks[moved]
        place = tx[g].at[vir, j, pl.ds(d * side, side), :]
        for lane, step in enumerate(order):
            peer, at = (vir + step) % vir_count, moved * len(order) + lane
            copy = pltpu.make_async_remote_copy(
                src_ref=t_ref.at[0, j, peer * tiles_here + g * depth + d], dst_ref=place,
                send_sem=m_send.at[at], recv_sem=m_recv.at[at],
                device_id=(occ, peer), device_id_type=MESH)
            copy.start()
            moves[g].append(copy)
        moves[g].append(keep(t_ref.at[0, j, vir * tiles_here + g * depth + d], place))
        moved += 1

    for copy in mine:
        copy.wait()
    pl.semaphore_wait(barrier, vir_count - 1 + len(occ_bits))
    z_stages = gather_stages(zall, occ, vir, occ_count, vir_count, z_send, z_recv)
    w_stages = gather_stages(wall, occ, vir, occ_count, vir_count, w_send, w_recv)
    wide = len(bits_down(vir_count))
    for at, stage in enumerate(z_stages):
        for copy in stage:
            copy.start()
        move_next()
        if at == 0:
            whole.start()
        if at >= wide:
            move_next()
        if at == len(z_stages) - 1:
            for _ in chunks:
                move_next()
        for copy in stage:
            copy.wait()

    def start_w(at):
        for copy in w_stages[at]:
            copy.start()

    def wait_w(at):
        for copy in w_stages[at]:
            copy.wait()

    start_w(0)
    backs = []
    for g in range(groups):
        for copy in moves[g]:
            copy.wait()

        def arrange(source, carry, g=g):
            for k in range(window):
                for col in range(here):
                    picks[k * tile_count + source * here + col] = tx[g][source, k, :, col * side:(col + 1) * side]
            return carry

        lax.fori_loop(0, vir_count, arrange, 0)

        def products(index, carry, g=g):
            j, dest = index // vir_count, index % vir_count
            for col in range(here):
                q = j * tile_count + dest * here + col
                picked, weights = [], []
                for m in range(cycle_keep):
                    picked.append(picks[cscreen_ref[q, m]])
                    slot = q * cycle_keep + m
                    weights.append(zall[slot // stored, (slot % stored) // sub, slot % sub])
                total = jnp.dot(
                    jnp.concatenate(picked, axis=1), jnp.concatenate(weights, axis=0),
                    preferred_element_type=jnp.float32)
                for d in range(depth):
                    kept = total[d * side:(d + 1) * side] * mask_ref[g * depth + d, q]
                    part[g][dest, j, d * side:(d + 1) * side, col * side:(col + 1) * side] = kept.astype(jnp.bfloat16)
            return carry

        lax.fori_loop(0, window * vir_count, products, 0)
        place = cycle_ref.at[:, pl.ds((vir * tiles_here + g * depth) * side, depth * side), :]
        for lane, step in enumerate(order):
            peer, at = (vir + step) % vir_count, g * len(order) + lane
            copy = pltpu.make_async_remote_copy(
                src_ref=part[g].at[peer], dst_ref=place, send_sem=b_send.at[at], recv_sem=b_recv.at[at],
                device_id=(occ, peer), device_id_type=MESH)
            copy.start()
            backs.append(copy)
        backs.append(keep(part[g].at[vir], place))
        wait_w(g)
        start_w(g + 1)

    for at in range(groups, len(w_stages)):
        wait_w(at)
        if at + 1 < len(w_stages):
            start_w(at + 1)
    whole.wait()

    batch = lad.shape[1]
    written = []
    for block in range(tile_count // batch):
        if block >= 2:
            written[block - 2].wait()

        def ladder_tile(index, carry, block=block):
            a = block * batch + index
            weights = []
            for k in range(ladder_keep):
                at = a * ladder_keep + k
                weights.append(wall[slot_ref[0, at], slot_ref[1, at], slot_ref[2, at]])
            weights = jnp.concatenate(weights, axis=1)
            for j in range(window):
                picked = jnp.concatenate([t_own[j, lscreen_ref[a, k]] for k in range(ladder_keep)], axis=0)
                lad[block % 2, index, j] = jnp.dot(weights, picked, preferred_element_type=jnp.float32)
            return carry

        lax.fori_loop(0, batch, ladder_tile, 0)
        copy = pltpu.make_async_copy(
            lad.at[block % 2], ladder_ref.at[pl.ds(block * batch, batch)], lad_sem.at[block])
        copy.start()
        written.append(copy)
    for copy in written[-2:]:
        copy.wait()
    for copy in backs:
        copy.wait()


def terms(ladder_screen, tile_slot, cycle_screen, used, tiled, ladder_tiles, cycle_tiles, occ_count, vir_count):
    _, window, tile_count, side, block_cols = tiled.shape
    stored = ladder_tiles.shape[0]
    groups, batch = 2, 8
    sub = stored // occ_count
    slots = jnp.stack([tile_slot // stored, (tile_slot % stored) // sub, tile_slot % sub])
    mask = jnp.broadcast_to(used.astype(jnp.float32)[:, :, None, None], used.shape + (1, side))
    tiles_here = tile_count // vir_count
    moves, gathers = tiles_here * window * (vir_count - 1), vir_count - 1 + occ_count - 1
    backs = groups * (vir_count - 1)
    group_shape = (vir_count, window, tiles_here // groups * side, block_cols)
    every = (vir_count, occ_count, stored // occ_count, side, side)
    smem, anywhere = pl.BlockSpec(memory_space=pltpu.SMEM), pl.BlockSpec(memory_space=pl.ANY)
    sems = [3 + tiles_here * window + groups, tile_count // batch,
            moves, moves, backs, backs, gathers, gathers, gathers, gathers]
    return pl.pallas_call(
        functools.partial(main_kernel, occ_count, vir_count),
        out_shape=(
            jax.ShapeDtypeStruct((window, tile_count * side, block_cols), jnp.bfloat16),
            jax.ShapeDtypeStruct((tile_count, window, side, block_cols), jnp.float32),
        ),
        in_specs=[smem] * 3 + [pl.BlockSpec(memory_space=pltpu.VMEM)] + [anywhere] * 3,
        out_specs=(anywhere,) * 2,
        scratch_shapes=[pltpu.VMEM(group_shape, jnp.bfloat16)] * (2 * groups) + [
            pltpu.VMEM(every, jnp.bfloat16),
            pltpu.VMEM(every, jnp.bfloat16),
            pltpu.VMEM((window, tile_count, side, block_cols), jnp.bfloat16),
            pltpu.VMEM((2, batch, window, side, block_cols), jnp.float32),
            pltpu.VMEM((window * tile_count, tiles_here // groups * side, side), jnp.bfloat16),
        ] + [pltpu.SemaphoreType.DMA((count,)) for count in sems],
        compiler_params=pltpu.CompilerParams(
            collective_id=0, has_side_effects=True, vmem_limit_bytes=VMEM_BYTES),
    )(ladder_screen, slots, cycle_screen, mask, tiled, ladder_tiles, cycle_tiles)


def update_kernel(energy_ref, row_ref, col_ref, near_ref, cycle_ref, ladder_ref, out_ref):
    tiles, window, side, _ = ladder_ref.shape
    for at in range(tiles):
        span = slice(at * side, (at + 1) * side)
        sums = row_ref[span] + col_ref[...] - energy_ref[0]
        for j in range(window):
            value = near_ref[0, j, span].astype(jnp.float32) + ladder_ref[at, j] + cycle_ref[j, span].astype(jnp.float32)
            out_ref[0, j, span] = (value / (sums - energy_ref[1 + j])).astype(jnp.bfloat16)


def update(energies, energy_a, energy_b, coulomb, cycle, ladder):
    tile_count, window, side, block_cols = ladder.shape
    tiles = 2
    block = pl.BlockSpec((1, window, tiles * side, block_cols), lambda a: (0, 0, a, 0))
    return pl.pallas_call(
        update_kernel,
        out_shape=jax.ShapeDtypeStruct(coulomb.shape, jnp.bfloat16),
        grid=(tile_count // tiles,),
        in_specs=[
            pl.BlockSpec(memory_space=pltpu.SMEM),
            pl.BlockSpec((tiles * side, 1), lambda a: (a, 0)),
            pl.BlockSpec((1, block_cols), lambda a: (0, 0)),
            block,
            pl.BlockSpec((window, tiles * side, block_cols), lambda a: (0, a, 0)),
            pl.BlockSpec((tiles, window, side, block_cols), lambda a: (a, 0, 0, 0)),
        ],
        out_specs=block,
        compiler_params=pltpu.CompilerParams(vmem_limit_bytes=VMEM_BYTES),
    )(energies, energy_a, energy_b, coulomb, cycle, ladder)


def body(
    amplitudes, coulomb, ladder_tiles, cycle_tiles, ladder_screen, tile_slot, cycle_screen,
    cycle_rows, cycle_count, slab_occ, window_occ, occ_energy, vir_energy,
):
    occ_count, vir_count = lax.axis_size("occ"), lax.axis_size("vir")
    slab_rows, window, width_all, block_cols = amplitudes.shape
    stored, side, _ = ladder_tiles.shape
    tile_count = width_all // side
    tiles_here = tile_count // vir_count
    occ, vir = lax.axis_index("occ"), lax.axis_index("vir")

    columns = lax.dynamic_slice_in_dim(cycle_rows, vir * tiles_here, tiles_here, 0)
    counts = lax.dynamic_slice_in_dim(cycle_count, vir * tiles_here, tiles_here, 0)
    listed = jnp.arange(columns.shape[1], dtype=jnp.int32)[None, :] < counts[:, None]
    every_q = jnp.arange(cycle_screen.shape[0], dtype=jnp.int32)
    used = jnp.any((columns[:, :, None] == every_q[None, None, :]) & listed[:, :, None], axis=1).astype(jnp.int32)

    orbital_ids = jnp.arange(occ_energy.shape[0], dtype=jnp.int32)
    wanted = jnp.concatenate([lax.dynamic_slice_in_dim(slab_occ, occ * slab_rows, slab_rows), window_occ])
    energies = jnp.sum(jnp.where(wanted[:, None] == orbital_ids[None, :], occ_energy[None, :], 0.0), axis=1)
    energy_a = vir_energy.reshape(width_all, 1)
    energy_b = lax.dynamic_slice_in_dim(vir_energy, vir * block_cols, block_cols).reshape(1, block_cols)

    tiled = amplitudes.reshape(slab_rows, window, tile_count, side, block_cols)
    cycle, ladder = terms(
        ladder_screen, tile_slot, cycle_screen, used, tiled, ladder_tiles, cycle_tiles, occ_count, vir_count)
    return update(energies, energy_a, energy_b, coulomb, cycle, ladder)


def solution(mesh):
    return jax.shard_map(
        body,
        mesh=mesh,
        in_specs=(
            P("occ", None, None, "vir"),
            P("occ", None, None, "vir"),
            P("vir", None, None),
            P("vir", None, None),
            P(), P(), P(), P(), P(), P(), P(), P(), P(),
        ),
        out_specs=P("occ", None, None, "vir"),
        check_vma=False,
    )
```

time: 470 us -> 449 us (0.955)
  Pallas kernels: 461 us -> 432 us
    pallas_call x4 -> x2, Pallas kernels: 461 us -> 432 us  [the longest x1 412 us: terms(): pl.pallas_call(functools.partial(main_kernel, occ_count, vir_count), out_...]
where the time goes in v3:
time: 449 us; the launch traced here: 446 us
  Pallas kernels  432 us (96%)
  local copies, waits for them, and re-layouts  9.81 us (2%)
    pallas_call x1, Pallas kernels, terms(): pl.pallas_call(functools.partial(main_kernel, occ_count, vir_count), out_...  412 us
    pallas_call x1, Pallas kernels, update(): pl.pallas_call(update_kernel, out_shape=jax.ShapeDtypeStruct(coulomb.shap...  20 us

profile of v3, /device:TPU:14, one launch (start us, length us, event | category | flops | bytes accessed | tf_op | source)
XLA Modules:
  0.0 445.8 jit_solution(15474222133388095885)
XLA Ops:
  0.0 0.0 copy-start
  0.0 1.2 dynamic_slice.12
  1.3 1.4 pad_add_fusion.1
  2.6 1.4 select_reduce_fusion.energy_ref
  4.0 0.7 dynamic_slice.15
  4.8 0.1 iota_compare_fusion.2
  4.8 0.0 copy-done
  4.8 0.1 fusion.1
  5.0 1.4 dynamic_slice.13
  6.3 0.7 and_select_fusion.3
  7.0 0.6 pad_add_fusion.slot_ref
  7.6 1.4 copy.19.lscreen_ref
  9.0 1.4 copy.20.cscreen_ref
  10.4 1.0 broadcast_in_dim.16.mask_ref
  11.4 2.8 copy.21.row_ref
  14.1 411.7 %shard_map.127 = (bf16[2,4096,512]{2,1,0:T(8,128)(2,1)}, f32[32,2,128,512]{3,2,1,0:T(8,128)}) custom-call(s32[32,8]{1,0:T(8,128)} %copy.19.lscreen_ref, s32[3,256]{1,0:T(4,128)} %pad_add_fusion.slot_ref, s32[64,4]{1,0:T(8,128)} %copy.20.cscreen_ref, f32[4,64,1,128]{3,2,1,0:T(1,128)} %broadcast_in_dim.16.mask_ref, bf16[1,2,32,128,512]{4,3,2,1,0:T(8,128)(2,1)} %bitcast.6, ...), custom_call_target="tpu_custom_call" | custom-call | tf_op jit(solution)/shard_map/pallas_call | solution.py:232
  425.8 20.0 %shard_map.128 = bf16[1,2,4096,512]{3,2,1,0:T(8,128)(2,1)} custom-call(f32[3]{0:T(128)} %select_reduce_fusion.energy_ref, f32[4096,1]{1,0:T(8,128)} %copy.21.row_ref, f32[1,512]{1,0:T(1,128)} %bitcast.8, bf16[1,2,4096,512]{3,2,1,0:T(8,128)(2,1)} %near_ref.1, bf16[2,4096,512]{2,1,0:T(8,128)(2,1)} %get-tuple-element.7.cycle_ref, ...), custom_call_target="tpu_custom_call" | custom-call | tf_op jit(solution)/shard_map/pallas_call | solution.py:266
  (2 shorter events, 0.0 us)
Async XLA Ops:
  0.0 4.8 %copy-start = (s32[32,48]{1,0:T(8,128)S(1)}, s32[32,48]{1,0:T(8,128)}, u32[]{:S(2)}) copy-start(s32[32,48]{1,0:T(8,128)} %param.20) | copy-start | bytes 18436

commit v4 on v3

--- a/solution.py
+++ b/solution.py
@@ -114,6 +114,7 @@
     w_stages = gather_stages(wall, occ, vir, occ_count, vir_count, w_send, w_recv)
     wide = len(bits_down(vir_count))
     for at, stage in enumerate(z_stages):
+        stage = stage + (w_stages[at] if at < wide else [])
         for copy in stage:
             copy.start()
         move_next()
@@ -135,7 +136,7 @@
         for copy in w_stages[at]:
             copy.wait()
 
-    start_w(0)
+    start_w(wide)
     backs = []
     for g in range(groups):
         for copy in moves[g]:
@@ -176,10 +177,12 @@
             copy.start()
             backs.append(copy)
         backs.append(keep(part[g].at[vir], place))
-        wait_w(g)
-        start_w(g + 1)
-
-    for at in range(groups, len(w_stages)):
+        if wide + g < len(w_stages):
+            wait_w(wide + g)
+        if wide + g + 1 < len(w_stages):
+            start_w(wide + g + 1)
+
+    for at in range(wide + groups, len(w_stages)):
         wait_w(at)
         if at + 1 < len(w_stages):
             start_w(at + 1)

time: 449 us -> 470 us (1.047)
  Pallas kernels: 432 us -> 453 us
    pallas_call x1, Pallas kernels: 412 us -> 433 us  [terms(): pl.pallas_call(functools.partial(main_kernel, occ_count, vir_count), out_...]
where the time goes in v4:
time: 470 us; the launch traced here: 467 us
  Pallas kernels  453 us (96%)
  local copies, waits for them, and re-layouts  9.81 us (2%)
    pallas_call x1, Pallas kernels, terms(): pl.pallas_call(functools.partial(main_kernel, occ_count, vir_count), out_...  433 us
    pallas_call x1, Pallas kernels, update(): pl.pallas_call(update_kernel, out_shape=jax.ShapeDtypeStruct(coulomb.shap...  20 us

profile of v4, /device:TPU:14, one launch (start us, length us, event | category | flops | bytes accessed | tf_op | source)
XLA Modules:
  0.0 467.4 jit_solution(2675469680149358827)
XLA Ops:
  0.0 0.0 copy-start
  0.0 1.2 dynamic_slice.12
  1.3 1.4 pad_add_fusion.1
  2.6 1.4 select_reduce_fusion.energy_ref
  4.0 0.7 dynamic_slice.15
  4.8 0.1 iota_compare_fusion.2
  4.8 0.0 copy-done
  4.8 0.1 fusion.1
  5.0 1.4 dynamic_slice.13
  6.3 0.7 and_select_fusion.3
  7.0 0.6 pad_add_fusion.slot_ref
  7.6 1.4 copy.19.lscreen_ref
  9.0 1.4 copy.20.cscreen_ref
  10.4 1.0 broadcast_in_dim.16.mask_ref
  11.4 2.8 copy.21.row_ref
  14.1 433.3 %shard_map.127 = (bf16[2,4096,512]{2,1,0:T(8,128)(2,1)}, f32[32,2,128,512]{3,2,1,0:T(8,128)}) custom-call(s32[32,8]{1,0:T(8,128)} %copy.19.lscreen_ref, s32[3,256]{1,0:T(4,128)} %pad_add_fusion.slot_ref, s32[64,4]{1,0:T(8,128)} %copy.20.cscreen_ref, f32[4,64,1,128]{3,2,1,0:T(1,128)} %broadcast_in_dim.16.mask_ref, bf16[1,2,32,128,512]{4,3,2,1,0:T(8,128)(2,1)} %bitcast.6, ...), custom_call_target="tpu_custom_call" | custom-call | tf_op jit(solution)/shard_map/pallas_call | solution.py:235
  447.4 20.0 %shard_map.128 = bf16[1,2,4096,512]{3,2,1,0:T(8,128)(2,1)} custom-call(f32[3]{0:T(128)} %select_reduce_fusion.energy_ref, f32[4096,1]{1,0:T(8,128)} %copy.21.row_ref, f32[1,512]{1,0:T(1,128)} %bitcast.8, bf16[1,2,4096,512]{3,2,1,0:T(8,128)(2,1)} %near_ref.1, bf16[2,4096,512]{2,1,0:T(8,128)(2,1)} %get-tuple-element.7.cycle_ref, ...), custom_call_target="tpu_custom_call" | custom-call | tf_op jit(solution)/shard_map/pallas_call | solution.py:269
  (2 shorter events, 0.0 us)
Async XLA Ops:
  0.0 4.8 %copy-start = (s32[32,48]{1,0:T(8,128)S(1)}, s32[32,48]{1,0:T(8,128)}, u32[]{:S(2)}) copy-start(s32[32,48]{1,0:T(8,128)} %param.20) | copy-start | bytes 18436
